TPU v7x, 256 devices: a whole 4x4x8 slice. The times are simulated.
256 devices in a mesh: lon: 16 (over z, core), lat: 16 (over y, x).
Axes of the slice: x: 4, y: 4, z: 8, core: 2. Of those that a mesh axis runs over, the one named last changes fastest.
Arguments:
- background: bfloat16 [64, 16, 256, 2048], P(None, None, 'lat', 'lon'), may hold values from -6 to 6
- ocean: int32 [256, 2048], P('lat', 'lon'), may hold values 0 or 1
- obs_level: int32 [16, 16, 2048], P('lat', 'lon'), may hold values from 0 to 15
- obs_row: int32 [16, 16, 2048], P('lat', 'lon'), may hold values from 0 to 16
- obs_col: int32 [16, 16, 2048], P('lat', 'lon'), may hold values from 0 to 128
- frac_row: float32 [16, 16, 2048], P('lat', 'lon'), may hold values from 0 to 1
- frac_col: float32 [16, 16, 2048], P('lat', 'lon'), may hold values from 0 to 1
- obs_value: float32 [16, 16, 2048], P('lat', 'lon'), may hold values from -8 to 8
- obs_error: float32 [16, 16, 2048], P('lat', 'lon'), may hold values from 1 to 10
- obs_flag: int32 [16, 16, 2048], P('lat', 'lon'), may hold values 0 or 1
Outputs:
- analysis: bfloat16 [64, 16, 256, 2048], P(None, None, 'lat', 'lon')
- departure: float32 [16, 16, 2048], P('lat', 'lon')
All inputs are finite; a program needn't handle non-finite values. No bound on the sum of `ocean` or of `obs_flag` on one device may be relied on, other than what follows from the above.
Results may differ from a plain program's by a relative error of at most 0.005.
Values may be sent and summed in bfloat16 or wider, within the bound.
A program may use at most 64 MiB of HBM per device.

v0:
```python
import functools
import math

import jax
import jax.numpy as jnp
from jax import lax
from jax.experimental import pallas as pl
from jax.experimental.pallas import tpu as pltpu
from jax.sharding import PartitionSpec as P

NS_ITERS = 6
INFLATION = 1.2

f32 = jnp.float32
bf16 = jnp.bfloat16
MESH = pl.DeviceIdType.MESH
SHIFTS = (-1, 0, 1)


def iota(shape, axis):
    return lax.broadcasted_iota(jnp.int32, shape, axis)


def dot(a, b):
    return jnp.dot(a, b, precision=lax.Precision.HIGHEST, preferred_element_type=f32)


def dot_t(a, b):
    return lax.dot_general(a, b, (((1,), (1,)), ((), ())), preferred_element_type=f32)


def observe(
    n_lon,
    n_lat,
    background,
    spot_any,
    row,
    col,
    frac_row,
    frac_col,
    value,
    error,
    flag,
    sums_out,
    departure,
    held,
    stage,
    edge,
    edge_in,
    table,
    side,
    side_in,
    spot,
    picked,
    pert,
    weighted,
    own,
    lon_in,
    lat_out,
    lat_in,
    load_sem,
    spot_sem,
    edge_send,
    edge_recv,
    side_send,
    side_recv,
    lon_send,
    lon_recv,
    lat_send,
    lat_recv,
):
    members, levels, depth, width = background.shape
    observations = spot.shape[0]
    stride = width + 8
    first = 8
    pairs = depth + 1
    at_lon, at_lat = lax.axis_index("lon"), lax.axis_index("lat")
    lon_at = {d: (lax.rem(at_lon + d + n_lon, n_lon), at_lat) for d in (-1, 1)}
    lat_at = {d: (at_lon, lax.rem(at_lat + d + n_lat, n_lat)) for d in (-1, 1)}

    chunks = load_sem.shape[0]
    each = levels // chunks
    loads = [
        pltpu.make_async_copy(
            background.at[:, pl.ds(c * each, each)],
            held.at[:, pl.ds(c * each, each)],
            load_sem.at[c],
        )
        for c in range(chunks)
    ]
    for load in loads:
        load.start()
    spot_load = pltpu.make_async_copy(spot_any, spot, spot_sem)
    spot_load.start()

    barrier = pltpu.get_barrier_semaphore()
    for there in (lon_at[-1], lon_at[1], lat_at[-1], lat_at[1]):
        pl.semaphore_signal(barrier, inc=1, device_id=there, device_id_type=MESH)
    pl.semaphore_wait(barrier, 4)

    def place(pair, level):
        return pl.multiple_of((pair * levels + level) * stride + first, 8)

    def turned(upper, lower):
        return jnp.concatenate([upper, lower], axis=0).astype(bf16).T.astype(f32)

    def build(level, carry):
        stage[...] = held[:, level].astype(f32).reshape(members * depth, width)
        rows = [stage[pl.ds(r, members, stride=depth), :] for r in range(depth)]
        here = pl.ds(pl.multiple_of(level * members, members), members)
        edge[0, here, :] = rows[0].astype(bf16)
        edge[1, here, :] = rows[depth - 1].astype(bf16)
        for pair in range(1, depth):
            table[pl.ds(place(pair, level), width), :] = turned(rows[pair - 1], rows[pair])
        return carry

    part = each * members
    edge_copies = []
    for c in range(chunks):
        loads[c].wait()
        lax.fori_loop(c * each, (c + 1) * each, build, 0)
        for index, toward in ((0, -1), (1, 1)):
            copy = pltpu.make_async_remote_copy(
                src_ref=edge.at[index, pl.ds(c * part, part)],
                dst_ref=edge_in.at[1 - index, pl.ds(c * part, part)],
                send_sem=edge_send.at[index, c],
                recv_sem=edge_recv.at[1 - index, c],
                device_id=lat_at[toward],
                device_id_type=MESH,
            )
            copy.start()
            edge_copies.append(copy)

    def side_copy(index, toward, begin, count, slot):
        return pltpu.make_async_remote_copy(
            src_ref=side.at[index, pl.ds(begin, count)],
            dst_ref=side_in.at[1 - index, pl.ds(begin, count)],
            send_sem=side_send.at[index, slot],
            recv_sem=side_recv.at[1 - index, slot],
            device_id=lon_at[toward],
            device_id_type=MESH,
        )

    total = pairs * levels
    inner = (depth - 1) * levels
    spans = ((levels, inner, levels, 0), (0, levels, 0, 1), (depth * levels, levels, depth * levels, 2))

    def send_sides(span):
        begin, count, _, slot = span
        copies = []
        for index, edge_col, toward in ((0, 0, -1), (1, width - 1, 1)):
            side[index, begin : begin + count, :] = table[
                pl.ds(begin * stride + first + edge_col, count, stride=stride), :
            ].astype(bf16)
            copy = side_copy(index, toward, begin, count, slot)
            copy.start()
            copies.append(copy)
        return copies

    side_copies = send_sides(spans[0])

    for copy in edge_copies:
        copy.wait()
    top = jnp.where(at_lat > 0, 1.0, 0.0).astype(f32)
    bottom = jnp.where(at_lat < n_lat - 1, 1.0, 0.0).astype(f32)

    def build_edges(level, carry):
        here = pl.ds(pl.multiple_of(level * members, members), members)
        north = edge_in[0, here, :].astype(f32) * top
        south = edge_in[1, here, :].astype(f32) * bottom
        table[pl.ds(place(0, level), width), :] = turned(north, edge[0, here, :].astype(f32))
        table[pl.ds(place(depth, level), width), :] = turned(edge[1, here, :].astype(f32), south)
        return carry

    lax.fori_loop(0, levels, build_edges, 0)
    side_copies += send_sides(spans[1]) + send_sides(spans[2])
    spot_load.wait()
    for copy in side_copies:
        copy.wait()
    table[pl.ds(first - 1, total, stride=stride), :] = side_in[0].astype(f32)
    table[pl.ds(stride, total, stride=stride), :] = side_in[1].astype(f32)

    def pick(o, carry):
        picked[pl.ds(o * 2, 2), :] = table[pl.ds(spot[o], 2), :]
        return carry

    lax.fori_loop(0, observations, pick, 0, unroll=16)

    pert[members:, :] = jnp.zeros((pert.shape[0] - members, observations), bf16)
    lanes = 128

    def block(b, carry):
        start = pl.multiple_of(b * lanes, lanes)
        here = pl.ds(start, lanes)
        corners = [
            picked[pl.ds(start * 2 + s, lanes, stride=2), :].astype(bf16).T.astype(f32)
            for s in range(2)
        ]
        fr, fc = frac_row[:, here], frac_col[:, here]
        model = (
            (1.0 - fr) * (1.0 - fc) * corners[0][:members]
            + (1.0 - fr) * fc * corners[1][:members]
            + fr * (1.0 - fc) * corners[0][members:]
            + fr * fc * corners[1][members:]
        )
        mean = jnp.sum(model, axis=0, keepdims=True) * (1.0 / members)
        rounded = (model - mean).astype(bf16)
        pert[:members, here] = rounded
        innov = value[:, here] - mean
        flags = flag[:, here].astype(f32)
        departure[:, here] = flags * innov
        pert[members : members + 16, here] = jnp.where(iota((16, lanes), 0) == 0, innov, 0.0).astype(
            bf16
        )
        gain = (flags / error[:, here]).astype(bf16).astype(f32)
        along = (col[:, here].astype(f32) - 0.5 + fc - width / 2).astype(bf16).astype(f32)
        across = (row[:, here].astype(f32) - 0.5 + fr - depth / 2).astype(bf16).astype(f32)
        values = rounded.astype(f32)
        for a in range(3):
            u = (along - SHIFTS[a] * width) / width
            for c in range(3):
                w = (across - SHIFTS[c] * depth) / depth
                weight = gain * jnp.exp(-0.5 * (u * u + w * w))
                weighted[a, c * members : (c + 1) * members, here] = (values * weight).astype(bf16)
        return carry

    lax.fori_loop(0, observations // lanes, block, 0)

    lon_copies = []
    for a, index, toward in ((0, 0, -1), (2, 1, 1)):
        own[a] = dot_t(weighted[a], pert[...])
        copy = pltpu.make_async_remote_copy(
            src_ref=own.at[a],
            dst_ref=lon_in.at[1 - index],
            send_sem=lon_send.at[index],
            recv_sem=lon_recv.at[1 - index],
            device_id=lon_at[toward],
            device_id_type=MESH,
        )
        copy.start()
        lon_copies.append(copy)
    middle = dot_t(weighted[1], pert[...])
    for copy in lon_copies:
        copy.wait()
    summed = middle + lon_in[0] + lon_in[1]
    lat_copies = []
    for c, index, toward in ((0, 0, -1), (2, 1, 1)):
        lat_out[index] = summed[c * members : (c + 1) * members]
        copy = pltpu.make_async_remote_copy(
            src_ref=lat_out.at[index],
            dst_ref=lat_in.at[1 - index],
            send_sem=lat_send.at[index],
            recv_sem=lat_recv.at[1 - index],
            device_id=lat_at[toward],
            device_id_type=MESH,
        )
        copy.start()
        lat_copies.append(copy)
    for copy in lat_copies:
        copy.wait()
    sums_out[...] = summed[members : 2 * members] + lat_in[0] * top + lat_in[1] * bottom


def transform_of(sums, members):
    eye = (iota((members, members), 0) == iota((members, members), 1)).astype(f32)
    system = (members - 1) / INFLATION * eye + sums[:, :members]
    squares = jnp.sum(system * system, axis=0, keepdims=True)
    scale = jnp.sqrt(jnp.sum(squares, axis=1, keepdims=True))
    upper = system / scale
    middle = 1.5 * eye - 0.5 * upper
    both = jnp.concatenate([dot(upper, middle), middle], axis=0)
    for step in range(1, NS_ITERS):
        middle = 1.5 * eye - 0.5 * dot(both[members:], both[:members])
        if step < NS_ITERS - 1:
            both = dot(both, middle)
        else:
            lower = dot(both[members:], middle)
    root = lower / jnp.sqrt(scale)
    mean_weights = dot(root, dot(root, sums))[:, members : members + 1]
    return (math.sqrt(members - 1) * root + mean_weights).astype(bf16)


def update(
    sums, ocean, departure, background, analysis, departure_out, held, result, spread_by, load_sem, store_sem
):
    members, levels, depth, width = background.shape
    n = members * depth
    chunks = load_sem.shape[0]
    each = levels // chunks
    loads = [
        pltpu.make_async_copy(
            background.at[:, pl.ds(c * each, each)],
            held.at[:, pl.ds(c * each, each)],
            load_sem.at[c],
        )
        for c in range(chunks)
    ]
    for load in loads:
        load.start()
    departure_out[...] = departure[...]
    transform = transform_of(sums[...], members)
    shift = depth.bit_length() - 1
    down = (jnp.right_shift(iota((n, members), 0), shift) == iota((n, members), 1)).astype(f32)
    along = (jnp.right_shift(iota((members, n), 1), shift) == iota((members, n), 0)).astype(f32)
    tall = dot_t(down.astype(bf16), transform).astype(bf16)
    part = 256
    for b in range(n // part):
        wide = jnp.dot(
            tall[b * part : (b + 1) * part], along.astype(bf16), preferred_element_type=f32
        )
        same = jnp.bitwise_and(iota((part, n), 0) - iota((part, n), 1), depth - 1) == 0
        spread_by[b * part : (b + 1) * part, :] = jnp.where(same, wide, 0.0).astype(bf16)
    for load in loads:
        load.wait()
    water = ocean[...] > 0
    at_once = 2

    def store(step):
        span = pl.ds(step * at_once, at_once)
        return pltpu.make_async_copy(result.at[:, span], analysis.at[:, span], store_sem.at[step])

    def levels_of(step, carry):
        base = step * at_once
        states = [held[:, base + j].astype(f32) for j in range(at_once)]
        means = [jnp.sum(state, axis=0) * (1.0 / members) for state in states]
        spread = jnp.concatenate(
            [(s - m[None]).astype(bf16).reshape(n, width) for s, m in zip(states, means)], axis=1
        )
        for b in range(n // part):
            mixed = jnp.dot(
                spread_by[b * part : (b + 1) * part, :], spread, preferred_element_type=f32
            )
            some = slice(b * (part // depth), (b + 1) * (part // depth))
            for j in range(at_once):
                change = mixed[:, j * width : (j + 1) * width].reshape(part // depth, depth, width)
                result[some, base + j] = jnp.where(
                    water[None], means[j][None] + change, held[some, base + j].astype(f32)
                ).astype(bf16)
        store(step).start()
        return carry

    lax.fori_loop(0, levels // at_once, levels_of, 0)
    for step in range(levels // at_once):
        store(step).wait()


def on_device(
    n_lon,
    n_lat,
    background,
    ocean,
    obs_level,
    obs_row,
    obs_col,
    frac_row,
    frac_col,
    obs_value,
    obs_error,
    obs_flag,
):
    members, levels, depth, width = background.shape
    observations = obs_level.shape[-1]
    stride = width + 8
    total = (depth + 1) * levels
    chunks = 4
    level, row, col = (x.reshape(-1) for x in (obs_level, obs_row, obs_col))
    spot = (row * levels + level) * stride + 7 + col
    lines = [
        x.reshape(1, observations)
        for x in (obs_row, obs_col, frac_row, frac_col, obs_value, obs_error, obs_flag)
    ]
    vmem = pl.BlockSpec(memory_space=pltpu.VMEM)
    anywhere = pl.BlockSpec(memory_space=pl.ANY)
    dma = pltpu.SemaphoreType.DMA
    sums, departure = pl.pallas_call(
        functools.partial(observe, n_lon, n_lat),
        out_shape=(
            jax.ShapeDtypeStruct((members, 128), f32),
            jax.ShapeDtypeStruct((1, observations), f32),
        ),
        in_specs=[anywhere, anywhere] + [vmem] * 7,
        out_specs=(vmem, vmem),
        scratch_shapes=[
            pltpu.VMEM(background.shape, bf16),
            pltpu.VMEM((members * depth, width), f32),
            pltpu.VMEM((2, levels * members, width), bf16),
            pltpu.VMEM((2, levels * members, width), bf16),
            pltpu.VMEM((total * stride + 8, 2 * members), f32),
            pltpu.VMEM((2, total, 2 * members), bf16),
            pltpu.VMEM((2, total, 2 * members), bf16),
            pltpu.SMEM((observations,), jnp.int32),
            pltpu.VMEM((2 * observations, 2 * members), f32),
            pltpu.VMEM((128, observations), bf16),
            pltpu.VMEM((3, 3 * members, observations), bf16),
            pltpu.VMEM((3, 3 * members, 128), f32),
            pltpu.VMEM((2, 3 * members, 128), f32),
            pltpu.VMEM((2, members, 128), f32),
            pltpu.VMEM((2, members, 128), f32),
            dma((chunks,)),
            dma,
            dma((2, chunks)),
            dma((2, chunks)),
            dma((2, 3)),
            dma((2, 3)),
            dma((2,)),
            dma((2,)),
            dma((2,)),
            dma((2,)),
        ],
        compiler_params=pltpu.CompilerParams(
            collective_id=0, has_side_effects=True, vmem_limit_bytes=48 << 20
        ),
        name="observe",
    )(background, spot, *lines)
    n = members * depth
    analysis, departure = pl.pallas_call(
        update,
        out_shape=(
            jax.ShapeDtypeStruct(background.shape, bf16),
            jax.ShapeDtypeStruct(departure.shape, f32),
        ),
        in_specs=[vmem, vmem, vmem, anywhere],
        out_specs=(anywhere, vmem),
        scratch_shapes=[
            pltpu.VMEM(background.shape, bf16),
            pltpu.VMEM(background.shape, bf16),
            pltpu.VMEM((n, n), bf16),
            dma((chunks,)),
            dma((levels // 2,)),
        ],
        compiler_params=pltpu.CompilerParams(vmem_limit_bytes=40 << 20),
        name="update",
    )(sums, ocean, departure, background)
    return analysis, departure.reshape(obs_value.shape)


def solution(mesh):
    here = P("lat", "lon", None)
    in_specs = (P(None, None, "lat", "lon"), P("lat", "lon")) + (here,) * 8
    out_specs = (P(None, None, "lat", "lon"), here)
    return jax.shard_map(
        functools.partial(on_device, mesh.shape["lon"], mesh.shape["lat"]),
        mesh=mesh,
        in_specs=in_specs,
        out_specs=out_specs,
        check_vma=False,
    )
```

profile of v0, /device:TPU:1, one launch (start us, length us, event | category | flops | bytes accessed | tf_op | source)
XLA Modules:
  0.0 57.0 jit_solution(5280181724472291497)
XLA Ops:
  0.6 0.0 copy-start.8
  0.6 0.8 %add_add_fusion = s32[1,1,2048]{2,1,0:T(1,128)S(1)} fusion(s32[1,1,2048]{2,1,0:T(1,128)} %param.14, s32[1,1,2048]{2,1,0:T(1,128)} %param.12, s32[1,1,2048]{2,1,0:T(1,128)} %param.13), kind=kLoop, calls=%fused_computation | loop fusion | flops 10240 | bytes 32768 | tf_op jit(solution)/shard_map/add | solution.py:367
  1.4 0.0 copy-start
  1.4 2.2 %copy-done = bf16[64,16,16,128]{3,2,1,0:T(8,128)(2,1)S(1)} copy-done((bf16[64,16,16,128]{3,2,1,0:T(8,128)(2,1)S(1)}, bf16[64,16,16,128]{3,2,1,0:T(8,128)(2,1)}, u32[]{:S(2)}) %copy-start) | copy-done | bytes 4194328
  3.6 0.0 copy-start.1
  3.6 0.7 %copy-done.1 = s32[1,1,2048]{2,1,0:T(1,128)S(1)} copy-done((s32[1,1,2048]{2,1,0:T(1,128)S(1)}, s32[1,1,2048]{2,1,0:T(1,128)}, u32[]{:S(2)}) %copy-start.1) | copy-done | bytes 8216
  4.3 0.0 copy-start.2
  4.3 0.7 %copy-done.2 = s32[1,1,2048]{2,1,0:T(1,128)S(1)} copy-done((s32[1,1,2048]{2,1,0:T(1,128)S(1)}, s32[1,1,2048]{2,1,0:T(1,128)}, u32[]{:S(2)}) %copy-start.2) | copy-done | bytes 8216
  5.0 0.0 copy-start.3
  5.0 0.7 %copy-done.3 = f32[1,1,2048]{2,1,0:T(1,128)S(1)} copy-done((f32[1,1,2048]{2,1,0:T(1,128)S(1)}, f32[1,1,2048]{2,1,0:T(1,128)}, u32[]{:S(2)}) %copy-start.3) | copy-done | bytes 8216
  5.7 0.0 copy-start.4
  5.7 0.7 %copy-done.4 = f32[1,1,2048]{2,1,0:T(1,128)S(1)} copy-done((f32[1,1,2048]{2,1,0:T(1,128)S(1)}, f32[1,1,2048]{2,1,0:T(1,128)}, u32[]{:S(2)}) %copy-start.4) | copy-done | bytes 8216
  6.4 0.0 copy-start.5
  6.4 0.7 %copy-done.5 = f32[1,1,2048]{2,1,0:T(1,128)S(1)} copy-done((f32[1,1,2048]{2,1,0:T(1,128)S(1)}, f32[1,1,2048]{2,1,0:T(1,128)}, u32[]{:S(2)}) %copy-start.5) | copy-done | bytes 8216
  7.1 0.0 copy-start.6
  7.1 0.7 %copy-done.6 = f32[1,1,2048]{2,1,0:T(1,128)S(1)} copy-done((f32[1,1,2048]{2,1,0:T(1,128)S(1)}, f32[1,1,2048]{2,1,0:T(1,128)}, u32[]{:S(2)}) %copy-start.6) | copy-done | bytes 8216
  7.8 0.0 copy-start.7
  7.8 0.7 %copy-done.7 = s32[1,1,2048]{2,1,0:T(1,128)S(1)} copy-done((s32[1,1,2048]{2,1,0:T(1,128)S(1)}, s32[1,1,2048]{2,1,0:T(1,128)}, u32[]{:S(2)}) %copy-start.7) | copy-done | bytes 8216
  8.5 35.8 %observe.1 = (f32[64,128]{1,0:T(8,128)S(1)}, f32[1,2048]{1,0:T(1,128)S(1)}) custom-call(bf16[64,16,16,128]{3,2,1,0:T(8,128)(2,1)S(1)} %copy-done, s32[2048]{0:T(1024)S(1)} %bitcast.11, s32[1,2048]{1,0:T(1,128)S(1)} %bitcast.10, s32[1,2048]{1,0:T(1,128)S(1)} %bitcast.9, f32[1,2048]{1,0:T(1,128)S(1)} %bitcast.12, f32[1,2048]{1,0:T(1,128)S(1)} %bitcast.13, ...), custom_call_target="tpu_custom_call" | custom-call | tf_op jit(solution)/shard_map/observe/pallas_call | solution.py:375
  44.3 0.0 copy-done.8
  44.3 12.7 %update.1 = (bf16[64,16,16,128]{3,2,1,0:T(8,128)(2,1)}, f32[1,2048]{1,0:T(1,128)}) custom-call(f32[64,128]{1,0:T(8,128)S(1)} %get-tuple-element.6.sums, s32[16,128]{1,0:T(8,128)S(1)} %copy-done.8, f32[1,2048]{1,0:T(1,128)S(1)} %get-tuple-element.7.departure, bf16[64,16,16,128]{3,2,1,0:T(8,128)(2,1)S(1)} %copy-done), custom_call_target="tpu_custom_call" | custom-call | tf_op jit(solution)/shard_map/update/pallas_call | solution.py:416
Async XLA Ops:
  0.6 43.7 %copy-start.8 = (s32[16,128]{1,0:T(8,128)S(1)}, s32[16,128]{1,0:T(8,128)}, u32[]{:S(2)}) copy-start(s32[16,128]{1,0:T(8,128)} %ocean.1) | copy-start | bytes 24580
  1.4 2.2 %copy-start = (bf16[64,16,16,128]{3,2,1,0:T(8,128)(2,1)S(1)}, bf16[64,16,16,128]{3,2,1,0:T(8,128)(2,1)}, u32[]{:S(2)}) copy-start(bf16[64,16,16,128]{3,2,1,0:T(8,128)(2,1)} %background.3) | copy-start | bytes 12582916
  3.6 0.7 %copy-start.1 = (s32[1,1,2048]{2,1,0:T(1,128)S(1)}, s32[1,1,2048]{2,1,0:T(1,128)}, u32[]{:S(2)}) copy-start(s32[1,1,2048]{2,1,0:T(1,128)} %param.14) | copy-start | bytes 24580
  4.3 0.7 %copy-start.2 = (s32[1,1,2048]{2,1,0:T(1,128)S(1)}, s32[1,1,2048]{2,1,0:T(1,128)}, u32[]{:S(2)}) copy-start(s32[1,1,2048]{2,1,0:T(1,128)} %param.13) | copy-start | bytes 24580
  5.0 0.7 %copy-start.3 = (f32[1,1,2048]{2,1,0:T(1,128)S(1)}, f32[1,1,2048]{2,1,0:T(1,128)}, u32[]{:S(2)}) copy-start(f32[1,1,2048]{2,1,0:T(1,128)} %param.15) | copy-start | bytes 24580
  5.7 0.7 %copy-start.4 = (f32[1,1,2048]{2,1,0:T(1,128)S(1)}, f32[1,1,2048]{2,1,0:T(1,128)}, u32[]{:S(2)}) copy-start(f32[1,1,2048]{2,1,0:T(1,128)} %param.16) | copy-start | bytes 24580
  6.4 0.7 %copy-start.5 = (f32[1,1,2048]{2,1,0:T(1,128)S(1)}, f32[1,1,2048]{2,1,0:T(1,128)}, u32[]{:S(2)}) copy-start(f32[1,1,2048]{2,1,0:T(1,128)} %param.17) | copy-start | bytes 24580
  7.1 0.7 %copy-start.6 = (f32[1,1,2048]{2,1,0:T(1,128)S(1)}, f32[1,1,2048]{2,1,0:T(1,128)}, u32[]{:S(2)}) copy-start(f32[1,1,2048]{2,1,0:T(1,128)} %param.18) | copy-start | bytes 24580
  7.8 0.7 %copy-start.7 = (s32[1,1,2048]{2,1,0:T(1,128)S(1)}, s32[1,1,2048]{2,1,0:T(1,128)}, u32[]{:S(2)}) copy-start(s32[1,1,2048]{2,1,0:T(1,128)} %param.19) | copy-start | bytes 24580
where the time goes:
time: 57.5 us; the launch traced here: 57 us
  Pallas kernels  48.5 us (84%)
  local copies, waits for them, and re-layouts  7.06 us (12%)
  other arithmetic  0.76 us (1%)
  between operations  0.67 us (1%)
    pallas_call x1, Pallas kernels, on_device(): pl.pallas_call(functools.partial(observe, n_lon, n_lat), out_shape=(jax.S...  35.8 us
    pallas_call x1, Pallas kernels, on_device(): pl.pallas_call(update, out_shape=(jax.ShapeDtypeStruct(background.shape,...  12.7 us
    unnamed x18, local copies, waits for them, and re-layouts  7.06 us

commit v1 on v0

v1 whole, which is shorter than its diff:
```python
import functools
import math

import jax
import jax.numpy as jnp
from jax import lax
from jax.experimental import pallas as pl
from jax.experimental.pallas import tpu as pltpu
from jax.sharding import PartitionSpec as P

NS_ITERS = 6
INFLATION = 1.2

f32 = jnp.float32
bf16 = jnp.bfloat16
MESH = pl.DeviceIdType.MESH
SHIFTS = (-1, 0, 1)


def iota(shape, axis):
    return lax.broadcasted_iota(jnp.int32, shape, axis)


def dot(a, b):
    return jnp.dot(a, b, precision=lax.Precision.HIGHEST, preferred_element_type=f32)


def dot_t(a, b):
    return lax.dot_general(a, b, (((1,), (1,)), ((), ())), preferred_element_type=f32)


def observe(
    n_lon,
    n_lat,
    background,
    level_in,
    row_in,
    col_in,
    frac_row_in,
    frac_col_in,
    value_in,
    error_in,
    flag_in,
    sums_out,
    departure,
    level,
    row,
    col,
    frac_row,
    frac_col,
    value,
    error,
    flag,
    spots,
    held,
    stage,
    edge,
    edge_in,
    table,
    side,
    side_in,
    corner_in,
    spot,
    picked,
    pert,
    weighted,
    own,
    sums_in,
    load_sem,
    line_sem,
    spot_sem,
    edge_send,
    edge_recv,
    side_send,
    side_recv,
    corner_send,
    corner_recv,
    sums_send,
    sums_recv,
):
    members, levels, depth, width = background.shape
    observations = spot.shape[1]
    stride = width + 8
    first = 8
    at_lon, at_lat = lax.axis_index("lon"), lax.axis_index("lat")

    def beside(lat, lon):
        return (lax.rem(at_lon + lon + n_lon, n_lon), lax.rem(at_lat + lat + n_lat, n_lat))

    def send(source, target, send_sem, recv_sem, lat, lon):
        copy = pltpu.make_async_remote_copy(
            src_ref=source,
            dst_ref=target,
            send_sem=send_sem,
            recv_sem=recv_sem,
            device_id=beside(lat, lon),
            device_id_type=MESH,
        )
        copy.start()
        return copy

    chunks = load_sem.shape[0]
    each = levels // chunks
    loads = [
        pltpu.make_async_copy(
            background.at[:, pl.ds(c * each, each)],
            held.at[:, pl.ds(c * each, each)],
            load_sem.at[c],
        )
        for c in range(chunks)
    ]
    for load in loads:
        load.start()
    lines = (level_in, row_in, col_in, frac_row_in, frac_col_in, value_in, error_in, flag_in)
    lines_held = (level, row, col, frac_row, frac_col, value, error, flag)
    line_loads = [
        pltpu.make_async_copy(there, here, line_sem.at[i])
        for i, (there, here) in enumerate(zip(lines, lines_held))
    ]
    for load in line_loads:
        load.start()

    around = [(lat, lon) for lat in SHIFTS for lon in SHIFTS if lat != 0 or lon != 0]
    barrier = pltpu.get_barrier_semaphore()
    for lat, lon in around:
        pl.semaphore_signal(barrier, inc=1, device_id=beside(lat, lon), device_id_type=MESH)
    pl.semaphore_wait(barrier, len(around))

    def place(pair, level):
        return pl.multiple_of((pair * levels + level) * stride + first, 8)

    def turned(upper, lower):
        return jnp.concatenate([upper, lower], axis=0).astype(bf16).T.astype(f32)

    def build(level, carry):
        stage[...] = held[:, level].astype(f32).reshape(members * depth, width)
        rows = [stage[pl.ds(r, members, stride=depth), :] for r in range(depth)]
        here = pl.ds(pl.multiple_of(level * members, members), members)
        edge[0, here, :] = rows[0].astype(bf16)
        edge[1, here, :] = rows[depth - 1].astype(bf16)
        for pair in range(1, depth):
            table[pl.ds(place(pair, level), width), :] = turned(rows[pair - 1], rows[pair])
        return carry

    part = each * members
    edge_copies = []
    for c in range(chunks):
        loads[c].wait()
        lax.fori_loop(c * each, (c + 1) * each, build, 0)
        span = pl.ds(c * part, part)
        edge_copies.append(
            [
                send(
                    edge.at[e, span],
                    edge_in.at[1 - e, span],
                    edge_send.at[e, c],
                    edge_recv.at[1 - e, c],
                    toward,
                    0,
                )
                for e, toward in ((0, -1), (1, 1))
            ]
        )

    inner = (depth - 1) * levels
    below = depth * levels * stride
    side_copies = []
    for s, toward in ((0, -1), (1, 1)):
        start = levels * stride + first + s * (width - 1)
        side[s] = table[pl.ds(start, inner, stride=stride), :].astype(bf16)
        for e, away in ((0, -1), (1, 1)):
            side_copies.append(
                send(
                    side.at[s, pl.ds(e * (inner - levels), levels)],
                    corner_in.at[1 - e, 1 - s],
                    corner_send.at[e, s],
                    corner_recv.at[1 - e, 1 - s],
                    away,
                    toward,
                )
            )
        side_copies.append(
            send(side.at[s], side_in.at[1 - s], side_send.at[s], side_recv.at[1 - s], 0, toward)
        )

    for load in line_loads:
        load.wait()
    spots[...] = (row[...] * levels + level[...]) * stride + (first - 1) + col[...]
    spot_load = pltpu.make_async_copy(spots, spot, spot_sem)
    spot_load.start()

    top = jnp.where(at_lat > 0, 1.0, 0.0).astype(f32)
    bottom = jnp.where(at_lat < n_lat - 1, 1.0, 0.0).astype(f32)

    def build_edges(level, carry):
        here = pl.ds(pl.multiple_of(level * members, members), members)
        north = edge_in[0, here, :].astype(f32) * top
        south = edge_in[1, here, :].astype(f32) * bottom
        table[pl.ds(place(0, level), width), :] = turned(north, edge[0, here, :].astype(f32))
        table[pl.ds(place(depth, level), width), :] = turned(edge[1, here, :].astype(f32), south)
        return carry

    for c in range(chunks):
        for copy in edge_copies[c]:
            copy.wait()
        lax.fori_loop(c * each, (c + 1) * each, build_edges, 0, unroll=each)
    spot_load.wait()
    for copy in side_copies:
        copy.wait()
    late = iota((levels, 2 * members), 1) >= members

    def swapped(x):
        return jnp.concatenate([x[:, members:], x[:, :members]], axis=1)

    for s in range(2):
        start = first - 1 + s * (width + 1)
        inside = side_in[s].astype(f32)
        above = jnp.where(late, corner_in[0, s].astype(f32) * top, inside[:levels])
        under = jnp.where(late, inside[inner - levels :], corner_in[1, s].astype(f32) * bottom)
        table[pl.ds(levels * stride + start, inner, stride=stride), :] = inside
        table[pl.ds(start, levels, stride=stride), :] = swapped(above)
        table[pl.ds(below + start, levels, stride=stride), :] = swapped(under)

    def pick(o, carry):
        picked[pl.ds(o * 2, 2), :] = table[pl.ds(spot[0, o], 2), :]
        return carry

    lax.fori_loop(0, observations, pick, 0, unroll=16)

    pert[members:, :] = jnp.zeros((pert.shape[0] - members, observations), bf16)
    lanes = 128

    def block(b, carry):
        start = pl.multiple_of(b * lanes, lanes)
        here = pl.ds(start, lanes)
        corners = [
            picked[pl.ds(start * 2 + s, lanes, stride=2), :].astype(bf16).T.astype(f32)
            for s in range(2)
        ]
        fr, fc = frac_row[:, here], frac_col[:, here]
        model = (
            (1.0 - fr) * (1.0 - fc) * corners[0][:members]
            + (1.0 - fr) * fc * corners[1][:members]
            + fr * (1.0 - fc) * corners[0][members:]
            + fr * fc * corners[1][members:]
        )
        mean = jnp.sum(model, axis=0, keepdims=True) * (1.0 / members)
        rounded = (model - mean).astype(bf16)
        pert[:members, here] = rounded
        innov = value[:, here] - mean
        flags = flag[:, here].astype(f32)
        departure[:, here] = flags * innov
        pert[members : members + 16, here] = jnp.where(iota((16, lanes), 0) == 0, innov, 0.0).astype(
            bf16
        )
        gain = (flags / error[:, here]).astype(bf16).astype(f32)
        along = (col[:, here].astype(f32) - 0.5 + fc - width / 2).astype(bf16).astype(f32)
        across = (row[:, here].astype(f32) - 0.5 + fr - depth / 2).astype(bf16).astype(f32)
        values = rounded.astype(f32)
        for a in range(3):
            u = (along - SHIFTS[a] * width) / width
            for c in range(3):
                w = (across - SHIFTS[c] * depth) / depth
                weight = gain * jnp.exp(-0.5 * (u * u + w * w))
                weighted[a, c * members : (c + 1) * members, here] = (values * weight).astype(bf16)
        return carry

    lax.fori_loop(0, observations // lanes, block, 0, unroll=2)

    sums_copies = []
    for a in (0, 2, 1):
        own[a] = dot_t(weighted[a], pert[...])
        for c in (0, 2, 1):
            if a != 1 or c != 1:
                sums_copies.append(
                    send(
                        own.at[a, pl.ds(c * members, members)],
                        sums_in.at[a, c],
                        sums_send.at[a, c],
                        sums_recv.at[a, c],
                        SHIFTS[c],
                        SHIFTS[a],
                    )
                )
    for copy in sums_copies:
        copy.wait()
    from_north = sums_in[0, 2] + sums_in[1, 2] + sums_in[2, 2]
    from_south = sums_in[0, 0] + sums_in[1, 0] + sums_in[2, 0]
    level_with = own[1, members : 2 * members, :] + sums_in[0, 1] + sums_in[2, 1]
    sums_out[...] = level_with + from_north * top + from_south * bottom


def transform_of(sums, members):
    eye = (iota((members, members), 0) == iota((members, members), 1)).astype(f32)
    system = (members - 1) / INFLATION * eye + sums[:, :members]
    squares = jnp.sum(system * system, axis=0, keepdims=True)
    scale = jnp.sqrt(jnp.sum(squares, axis=1, keepdims=True))
    upper = system / scale
    middle = 1.5 * eye - 0.5 * upper
    both = jnp.concatenate([dot(upper, middle), middle], axis=0)
    for step in range(1, NS_ITERS):
        middle = 1.5 * eye - 0.5 * dot(both[members:], both[:members])
        if step < NS_ITERS - 1:
            both = dot(both, middle)
        else:
            lower = dot(both[members:], middle)
    root = lower / jnp.sqrt(scale)
    mean_weights = dot(root, dot(root, sums))[:, members : members + 1]
    return (math.sqrt(members - 1) * root + mean_weights).astype(bf16)


def update(
    sums, ocean, departure, background, analysis, departure_out, held, result, spread_by, load_sem, store_sem
):
    members, levels, depth, width = background.shape
    half = 8
    halves = depth // half
    n = members * half
    chunks = load_sem.shape[0]
    each = members // chunks
    loads = [
        pltpu.make_async_copy(
            background.at[pl.ds(c * each, each)], held.at[pl.ds(c * each, each)], load_sem.at[c]
        )
        for c in range(chunks)
    ]
    for load in loads:
        load.start()
    departure_out[...] = departure[...]
    transform = transform_of(sums[...], members)
    shift = half.bit_length() - 1
    down = (jnp.right_shift(iota((n, members), 0), shift) == iota((n, members), 1)).astype(f32)
    along = (jnp.right_shift(iota((members, n), 1), shift) == iota((members, n), 0)).astype(f32)
    tall = dot_t(down.astype(bf16), transform).astype(bf16)
    wide = jnp.dot(tall, along.astype(bf16), preferred_element_type=f32)
    same = jnp.bitwise_and(iota((n, n), 0) - iota((n, n), 1), half - 1) == 0
    spread_by[...] = jnp.where(same, wide, 0.0).astype(bf16)
    for load in loads:
        load.wait()
    water = ocean[...] > 0
    at_once = 2

    def store(step):
        span = pl.ds(step * at_once, at_once)
        return pltpu.make_async_copy(result.at[:, span], analysis.at[:, span], store_sem.at[step])

    def one_level(level):
        state = held[:, level].astype(f32)
        mean = jnp.sum(state, axis=0) * (1.0 / members)
        spread = state - mean[None]
        spread = jnp.concatenate(
            [
                spread[:, h * half : (h + 1) * half].reshape(n, width).astype(bf16)
                for h in range(halves)
            ],
            axis=1,
        )
        mixed = jnp.dot(spread_by[...], spread, preferred_element_type=f32)
        change = jnp.concatenate(
            [
                mixed[:, h * width : (h + 1) * width].reshape(members, half, width)
                for h in range(halves)
            ],
            axis=1,
        )
        result[:, level] = jnp.where(
            water[None], mean[None] + change, held[:, level].astype(f32)
        ).astype(bf16)

    def some_levels(step, carry):
        for j in range(at_once):
            one_level(step * at_once + j)
        store(step).start()
        return carry

    lax.fori_loop(0, levels // at_once, some_levels, 0, unroll=2)
    for step in range(levels // at_once):
        store(step).wait()


def on_device(
    n_lon,
    n_lat,
    background,
    ocean,
    obs_level,
    obs_row,
    obs_col,
    frac_row,
    frac_col,
    obs_value,
    obs_error,
    obs_flag,
):
    members, levels, depth, width = background.shape
    observations = obs_level.shape[-1]
    stride = width + 8
    total = (depth + 1) * levels
    inner = (depth - 1) * levels
    chunks = math.gcd(levels, 8)
    lines = [
        x.reshape(1, observations)
        for x in (obs_level, obs_row, obs_col, frac_row, frac_col, obs_value, obs_error, obs_flag)
    ]
    vmem = pl.BlockSpec(memory_space=pltpu.VMEM)
    anywhere = pl.BlockSpec(memory_space=pl.ANY)
    dma = pltpu.SemaphoreType.DMA
    sums, departure = pl.pallas_call(
        functools.partial(observe, n_lon, n_lat),
        out_shape=(
            jax.ShapeDtypeStruct((members, 128), f32),
            jax.ShapeDtypeStruct((1, observations), f32),
        ),
        in_specs=[anywhere] * 9,
        out_specs=(vmem, vmem),
        scratch_shapes=[pltpu.VMEM(line.shape, line.dtype) for line in lines]
        + [
            pltpu.VMEM((1, observations), jnp.int32),
            pltpu.VMEM(background.shape, bf16),
            pltpu.VMEM((members * depth, width), f32),
            pltpu.VMEM((2, levels * members, width), bf16),
            pltpu.VMEM((2, levels * members, width), bf16),
            pltpu.VMEM((total * stride + 8, 2 * members), f32),
            pltpu.VMEM((2, inner, 2 * members), bf16),
            pltpu.VMEM((2, inner, 2 * members), bf16),
            pltpu.VMEM((2, 2, levels, 2 * members), bf16),
            pltpu.SMEM((1, observations), jnp.int32),
            pltpu.VMEM((2 * observations, 2 * members), f32),
            pltpu.VMEM((128, observations), bf16),
            pltpu.VMEM((3, 3 * members, observations), bf16),
            pltpu.VMEM((3, 3 * members, 128), f32),
            pltpu.VMEM((3, 3, members, 128), f32),
            dma((chunks,)),
            dma((8,)),
            dma,
            dma((2, chunks)),
            dma((2, chunks)),
            dma((2,)),
            dma((2,)),
            dma((2, 2)),
            dma((2, 2)),
            dma((3, 3)),
            dma((3, 3)),
        ],
        compiler_params=pltpu.CompilerParams(
            collective_id=0, has_side_effects=True, vmem_limit_bytes=48 << 20
        ),
        name="observe",
    )(background, *lines)
    n = members * 8
    analysis, departure = pl.pallas_call(
        update,
        out_shape=(
            jax.ShapeDtypeStruct(background.shape, bf16),
            jax.ShapeDtypeStruct(departure.shape, f32),
        ),
        in_specs=[vmem, vmem, vmem, anywhere],
        out_specs=(anywhere, vmem),
        scratch_shapes=[
            pltpu.VMEM(background.shape, bf16),
            pltpu.VMEM(background.shape, bf16),
            pltpu.VMEM((n, n), bf16),
            dma((8,)),
            dma((levels // 2,)),
        ],
        compiler_params=pltpu.CompilerParams(vmem_limit_bytes=40 << 20),
        name="update",
    )(sums, ocean, departure, background)
    return analysis, departure.reshape(obs_value.shape)


def solution(mesh):
    here = P("lat", "lon", None)
    in_specs = (P(None, None, "lat", "lon"), P("lat", "lon")) + (here,) * 8
    out_specs = (P(None, None, "lat", "lon"), here)
    return jax.shard_map(
        functools.partial(on_device, mesh.shape["lon"], mesh.shape["lat"]),
        mesh=mesh,
        in_specs=in_specs,
        out_specs=out_specs,
        check_vma=False,
    )
```

time: 57.5 us -> 48 us (0.83)
  Pallas kernels: 48.5 us -> 39 us
  other arithmetic: 0.76 us -> 0 us
  local copies, waits for them, and re-layouts: 7.06 us -> 7.76 us
    pallas_call x1, Pallas kernels: 35.8 us -> 30.7 us  [on_device(): pl.pallas_call(functools.partial(observe, n_lon, n_lat), out_shape=(jax.S...]
    pallas_call x1, Pallas kernels: 12.7 us -> 8.28 us  [on_device(): pl.pallas_call(update, out_shape=(jax.ShapeDtypeStruct(background.shape,...]
    add x1 -> x0, other arithmetic: 0.76 us -> none  [on_device(): spot = (row * levels + level) * stride + 7 + col]
    unnamed x18 -> x20, local copies, waits for them, and re-layouts: 7.06 us -> 7.76 us
where the time goes in v1:
time: 48 us; the launch traced here: 47.4 us
  Pallas kernels  39 us (81%)
  local copies, waits for them, and re-layouts  7.76 us (16%)
  between operations  0.67 us (1%)
    pallas_call x1, Pallas kernels, on_device(): pl.pallas_call(functools.partial(observe, n_lon, n_lat), out_shape=(jax.S...  30.7 us
    pallas_call x1, Pallas kernels, on_device(): pl.pallas_call(update, out_shape=(jax.ShapeDtypeStruct(background.shape,...  8.28 us
    unnamed x20, local copies, waits for them, and re-layouts  7.76 us

profile of v1, /device:TPU:1, one launch (start us, length us, event | category | flops | bytes accessed | tf_op | source)
XLA Modules:
  0.0 47.4 jit_solution(6259957683488023389)
XLA Ops:
  0.6 0.0 copy-start.9
  0.6 0.0 copy-start
  0.7 2.2 %copy-done = bf16[64,16,16,128]{3,2,1,0:T(8,128)(2,1)S(1)} copy-done((bf16[64,16,16,128]{3,2,1,0:T(8,128)(2,1)S(1)}, bf16[64,16,16,128]{3,2,1,0:T(8,128)(2,1)}, u32[]{:S(2)}) %copy-start) | copy-done | bytes 4194328
  2.8 0.0 copy-start.1
  2.8 0.7 %copy-done.1 = s32[1,1,2048]{2,1,0:T(1,128)S(1)} copy-done((s32[1,1,2048]{2,1,0:T(1,128)S(1)}, s32[1,1,2048]{2,1,0:T(1,128)}, u32[]{:S(2)}) %copy-start.1) | copy-done | bytes 8216
  3.5 0.0 copy-start.2
  3.5 0.7 %copy-done.2 = s32[1,1,2048]{2,1,0:T(1,128)S(1)} copy-done((s32[1,1,2048]{2,1,0:T(1,128)S(1)}, s32[1,1,2048]{2,1,0:T(1,128)}, u32[]{:S(2)}) %copy-start.2) | copy-done | bytes 8216
  4.2 0.0 copy-start.3
  4.2 0.7 %copy-done.3 = s32[1,1,2048]{2,1,0:T(1,128)S(1)} copy-done((s32[1,1,2048]{2,1,0:T(1,128)S(1)}, s32[1,1,2048]{2,1,0:T(1,128)}, u32[]{:S(2)}) %copy-start.3) | copy-done | bytes 8216
  4.9 0.0 copy-start.4
  4.9 0.7 %copy-done.4 = f32[1,1,2048]{2,1,0:T(1,128)S(1)} copy-done((f32[1,1,2048]{2,1,0:T(1,128)S(1)}, f32[1,1,2048]{2,1,0:T(1,128)}, u32[]{:S(2)}) %copy-start.4) | copy-done | bytes 8216
  5.6 0.0 copy-start.5
  5.6 0.7 %copy-done.5 = f32[1,1,2048]{2,1,0:T(1,128)S(1)} copy-done((f32[1,1,2048]{2,1,0:T(1,128)S(1)}, f32[1,1,2048]{2,1,0:T(1,128)}, u32[]{:S(2)}) %copy-start.5) | copy-done | bytes 8216
  6.3 0.0 copy-start.6
  6.3 0.7 %copy-done.6 = f32[1,1,2048]{2,1,0:T(1,128)S(1)} copy-done((f32[1,1,2048]{2,1,0:T(1,128)S(1)}, f32[1,1,2048]{2,1,0:T(1,128)}, u32[]{:S(2)}) %copy-start.6) | copy-done | bytes 8216
  7.0 0.0 copy-start.7
  7.0 0.7 %copy-done.7 = f32[1,1,2048]{2,1,0:T(1,128)S(1)} copy-done((f32[1,1,2048]{2,1,0:T(1,128)S(1)}, f32[1,1,2048]{2,1,0:T(1,128)}, u32[]{:S(2)}) %copy-start.7) | copy-done | bytes 8216
  7.7 0.0 copy-start.8
  7.7 0.7 %copy-done.8 = s32[1,1,2048]{2,1,0:T(1,128)S(1)} copy-done((s32[1,1,2048]{2,1,0:T(1,128)S(1)}, s32[1,1,2048]{2,1,0:T(1,128)}, u32[]{:S(2)}) %copy-start.8) | copy-done | bytes 8216
  8.4 30.7 %observe.1 = (f32[64,128]{1,0:T(8,128)S(1)}, f32[1,2048]{1,0:T(1,128)S(1)}) custom-call(bf16[64,16,16,128]{3,2,1,0:T(8,128)(2,1)S(1)} %copy-done, s32[1,2048]{1,0:T(1,128)S(1)} %bitcast.9, s32[1,2048]{1,0:T(1,128)S(1)} %bitcast.10, s32[1,2048]{1,0:T(1,128)S(1)} %bitcast.11, f32[1,2048]{1,0:T(1,128)S(1)} %bitcast.12, f32[1,2048]{1,0:T(1,128)S(1)} %bitcast.13, ...), custom_call_target="tpu_custom_call" | custom-call | tf_op jit(solution)/shard_map/observe/pallas_call | solution.py:408
  39.2 0.0 copy-done.9
  39.2 8.3 %update.1 = (bf16[64,16,16,128]{3,2,1,0:T(8,128)(2,1)}, f32[1,2048]{1,0:T(1,128)}) custom-call(f32[64,128]{1,0:T(8,128)S(1)} %get-tuple-element.6.sums, s32[16,128]{1,0:T(8,128)S(1)} %copy-done.9, f32[1,2048]{1,0:T(1,128)S(1)} %get-tuple-element.7.departure, bf16[64,16,16,128]{3,2,1,0:T(8,128)(2,1)S(1)} %copy-done), custom_call_target="tpu_custom_call" | custom-call | tf_op jit(solution)/shard_map/update/pallas_call | solution.py:451
Async XLA Ops:
  0.6 38.5 %copy-start.9 = (s32[16,128]{1,0:T(8,128)S(1)}, s32[16,128]{1,0:T(8,128)}, u32[]{:S(2)}) copy-start(s32[16,128]{1,0:T(8,128)} %ocean.1) | copy-start | bytes 24580
  0.6 2.2 %copy-start = (bf16[64,16,16,128]{3,2,1,0:T(8,128)(2,1)S(1)}, bf16[64,16,16,128]{3,2,1,0:T(8,128)(2,1)}, u32[]{:S(2)}) copy-start(bf16[64,16,16,128]{3,2,1,0:T(8,128)(2,1)} %background.3) | copy-start | bytes 12582916
  2.8 0.7 %copy-start.1 = (s32[1,1,2048]{2,1,0:T(1,128)S(1)}, s32[1,1,2048]{2,1,0:T(1,128)}, u32[]{:S(2)}) copy-start(s32[1,1,2048]{2,1,0:T(1,128)} %param.12) | copy-start | bytes 24580
  3.5 0.7 %copy-start.2 = (s32[1,1,2048]{2,1,0:T(1,128)S(1)}, s32[1,1,2048]{2,1,0:T(1,128)}, u32[]{:S(2)}) copy-start(s32[1,1,2048]{2,1,0:T(1,128)} %param.13) | copy-start | bytes 24580
  4.2 0.7 %copy-start.3 = (s32[1,1,2048]{2,1,0:T(1,128)S(1)}, s32[1,1,2048]{2,1,0:T(1,128)}, u32[]{:S(2)}) copy-start(s32[1,1,2048]{2,1,0:T(1,128)} %param.14) | copy-start | bytes 24580
  4.9 0.7 %copy-start.4 = (f32[1,1,2048]{2,1,0:T(1,128)S(1)}, f32[1,1,2048]{2,1,0:T(1,128)}, u32[]{:S(2)}) copy-start(f32[1,1,2048]{2,1,0:T(1,128)} %param.15) | copy-start | bytes 24580
  5.6 0.7 %copy-start.5 = (f32[1,1,2048]{2,1,0:T(1,128)S(1)}, f32[1,1,2048]{2,1,0:T(1,128)}, u32[]{:S(2)}) copy-start(f32[1,1,2048]{2,1,0:T(1,128)} %param.16) | copy-start | bytes 24580
  6.3 0.7 %copy-start.6 = (f32[1,1,2048]{2,1,0:T(1,128)S(1)}, f32[1,1,2048]{2,1,0:T(1,128)}, u32[]{:S(2)}) copy-start(f32[1,1,2048]{2,1,0:T(1,128)} %param.17) | copy-start | bytes 24580
  7.0 0.7 %copy-start.7 = (f32[1,1,2048]{2,1,0:T(1,128)S(1)}, f32[1,1,2048]{2,1,0:T(1,128)}, u32[]{:S(2)}) copy-start(f32[1,1,2048]{2,1,0:T(1,128)} %param.18) | copy-start | bytes 24580
  7.7 0.7 %copy-start.8 = (s32[1,1,2048]{2,1,0:T(1,128)S(1)}, s32[1,1,2048]{2,1,0:T(1,128)}, u32[]{:S(2)}) copy-start(s32[1,1,2048]{2,1,0:T(1,128)} %param.19) | copy-start | bytes 24580

commit v2 on v1

--- a/solution.py
+++ b/solution.py
@@ -52,6 +52,7 @@
     error,
     flag,
     spots,
+    shares,
     held,
     stage,
     edge,
@@ -59,6 +60,7 @@
     table,
     side,
     side_in,
+    corner,
     corner_in,
     spot,
     picked,
@@ -100,12 +102,10 @@
         return copy
 
     chunks = load_sem.shape[0]
-    each = levels // chunks
+    each = members // chunks
     loads = [
         pltpu.make_async_copy(
-            background.at[:, pl.ds(c * each, each)],
-            held.at[:, pl.ds(c * each, each)],
-            load_sem.at[c],
+            background.at[pl.ds(c * each, each)], held.at[pl.ds(c * each, each)], load_sem.at[c]
         )
         for c in range(chunks)
     ]
@@ -124,7 +124,6 @@
     barrier = pltpu.get_barrier_semaphore()
     for lat, lon in around:
         pl.semaphore_signal(barrier, inc=1, device_id=beside(lat, lon), device_id_type=MESH)
-    pl.semaphore_wait(barrier, len(around))
 
     def place(pair, level):
         return pl.multiple_of((pair * levels + level) * stride + first, 8)
@@ -132,22 +131,30 @@
     def turned(upper, lower):
         return jnp.concatenate([upper, lower], axis=0).astype(bf16).T.astype(f32)
 
-    def build(level, carry):
-        stage[...] = held[:, level].astype(f32).reshape(members * depth, width)
-        rows = [stage[pl.ds(r, members, stride=depth), :] for r in range(depth)]
-        here = pl.ds(pl.multiple_of(level * members, members), members)
-        edge[0, here, :] = rows[0].astype(bf16)
-        edge[1, here, :] = rows[depth - 1].astype(bf16)
-        for pair in range(1, depth):
-            table[pl.ds(place(pair, level), width), :] = turned(rows[pair - 1], rows[pair])
-        return carry
-
-    part = each * members
-    edge_copies = []
+    def put(pair, level, upper, lower):
+        table[pl.ds(place(pair, level), width), :] = turned(upper, lower)
+
     for c in range(chunks):
         loads[c].wait()
-        lax.fori_loop(c * each, (c + 1) * each, build, 0)
-        span = pl.ds(c * part, part)
+
+        def lay_out(level, carry):
+            begin = c * each * depth
+            some = held[c * each : (c + 1) * each, level].astype(f32)
+            stage[level, begin : begin + each * depth, :] = some.reshape(each * depth, width)
+            here = pl.ds(pl.multiple_of(level * members + c * each, each), each)
+            for e in range(2):
+                line = stage[level, pl.ds(begin + e * (depth - 1), each, stride=depth), :]
+                edge[e, here, :] = line.astype(bf16)
+            return carry
+
+        lax.fori_loop(0, levels, lay_out, 0, unroll=4)
+
+    pl.semaphore_wait(barrier, len(around))
+    parts = edge_send.shape[1]
+    part = levels // parts
+    edge_copies = []
+    for c in range(parts):
+        span = pl.ds(c * part * members, part * members)
         edge_copies.append(
             [
                 send(
@@ -162,16 +169,26 @@
             ]
         )
 
+    def line_of(level, r):
+        return stage[level, pl.ds(r, members, stride=depth), :]
+
+    def build_outer(level, carry):
+        put(1, level, line_of(level, 0), line_of(level, 1))
+        put(depth - 1, level, line_of(level, depth - 2), line_of(level, depth - 1))
+        return carry
+
+    lax.fori_loop(0, levels, build_outer, 0, unroll=4)
+
     inner = (depth - 1) * levels
     below = depth * levels * stride
     side_copies = []
-    for s, toward in ((0, -1), (1, 1)):
-        start = levels * stride + first + s * (width - 1)
-        side[s] = table[pl.ds(start, inner, stride=stride), :].astype(bf16)
-        for e, away in ((0, -1), (1, 1)):
+    for e, away in ((0, -1), (1, 1)):
+        for s, toward in ((0, -1), (1, 1)):
+            start = (levels + e * (inner - levels)) * stride + first + s * (width - 1)
+            corner[e, s] = table[pl.ds(start, levels, stride=stride), :].astype(bf16)
             side_copies.append(
                 send(
-                    side.at[s, pl.ds(e * (inner - levels), levels)],
+                    corner.at[e, s],
                     corner_in.at[1 - e, 1 - s],
                     corner_send.at[e, s],
                     corner_recv.at[1 - e, 1 - s],
@@ -179,6 +196,18 @@
                     toward,
                 )
             )
+
+    def build(level, carry):
+        rows = [line_of(level, r) for r in range(1, depth - 1)]
+        for pair in range(2, depth - 1):
+            put(pair, level, rows[pair - 2], rows[pair - 1])
+        return carry
+
+    lax.fori_loop(0, levels, build, 0, unroll=2)
+
+    for s, toward in ((0, -1), (1, 1)):
+        start = levels * stride + first + s * (width - 1)
+        side[s] = table[pl.ds(start, inner, stride=stride), :].astype(bf16)
         side_copies.append(
             send(side.at[s], side_in.at[1 - s], side_send.at[s], side_recv.at[1 - s], 0, toward)
         )
@@ -188,6 +217,21 @@
     spots[...] = (row[...] * levels + level[...]) * stride + (first - 1) + col[...]
     spot_load = pltpu.make_async_copy(spots, spot, spot_sem)
     spot_load.start()
+    fr, fc = frac_row[...], frac_col[...]
+    for k, share in enumerate(
+        ((1.0 - fr) * (1.0 - fc), (1.0 - fr) * fc, fr * (1.0 - fc), fr * fc)
+    ):
+        shares[k : k + 1, :] = share
+    flags = flag[...].astype(f32)
+    gain = (flags / error[...]).astype(bf16).astype(f32)
+    along = (col[...].astype(f32) - 0.5 + fc - width / 2).astype(bf16).astype(f32)
+    across = (row[...].astype(f32) - 0.5 + fr - depth / 2).astype(bf16).astype(f32)
+    for a in range(3):
+        u = (along - SHIFTS[a] * width) / width
+        for c in range(3):
+            w = (across - SHIFTS[c] * depth) / depth
+            k = 4 + a * 3 + c
+            shares[k : k + 1, :] = gain * jnp.exp(-0.5 * (u * u + w * w))
 
     top = jnp.where(at_lat > 0, 1.0, 0.0).astype(f32)
     bottom = jnp.where(at_lat < n_lat - 1, 1.0, 0.0).astype(f32)
@@ -196,14 +240,14 @@
         here = pl.ds(pl.multiple_of(level * members, members), members)
         north = edge_in[0, here, :].astype(f32) * top
         south = edge_in[1, here, :].astype(f32) * bottom
-        table[pl.ds(place(0, level), width), :] = turned(north, edge[0, here, :].astype(f32))
-        table[pl.ds(place(depth, level), width), :] = turned(edge[1, here, :].astype(f32), south)
+        put(0, level, north, line_of(level, 0))
+        put(depth, level, line_of(level, depth - 1), south)
         return carry
 
-    for c in range(chunks):
+    for c in range(parts):
         for copy in edge_copies[c]:
             copy.wait()
-        lax.fori_loop(c * each, (c + 1) * each, build_edges, 0, unroll=each)
+        lax.fori_loop(c * part, (c + 1) * part, build_edges, 0, unroll=part)
     spot_load.wait()
     for copy in side_copies:
         copy.wait()
@@ -227,49 +271,42 @@
 
     lax.fori_loop(0, observations, pick, 0, unroll=16)
 
-    pert[members:, :] = jnp.zeros((pert.shape[0] - members, observations), bf16)
     lanes = 128
 
     def block(b, carry):
         start = pl.multiple_of(b * lanes, lanes)
         here = pl.ds(start, lanes)
-        corners = [
+        left, right = (
             picked[pl.ds(start * 2 + s, lanes, stride=2), :].astype(bf16).T.astype(f32)
             for s in range(2)
-        ]
-        fr, fc = frac_row[:, here], frac_col[:, here]
+        )
         model = (
-            (1.0 - fr) * (1.0 - fc) * corners[0][:members]
-            + (1.0 - fr) * fc * corners[1][:members]
-            + fr * (1.0 - fc) * corners[0][members:]
-            + fr * fc * corners[1][members:]
+            shares[0:1, here] * left[:members]
+            + shares[1:2, here] * right[:members]
+            + shares[2:3, here] * left[members:]
+            + shares[3:4, here] * right[members:]
         )
         mean = jnp.sum(model, axis=0, keepdims=True) * (1.0 / members)
         rounded = (model - mean).astype(bf16)
-        pert[:members, here] = rounded
         innov = value[:, here] - mean
-        flags = flag[:, here].astype(f32)
-        departure[:, here] = flags * innov
-        pert[members : members + 16, here] = jnp.where(iota((16, lanes), 0) == 0, innov, 0.0).astype(
-            bf16
-        )
-        gain = (flags / error[:, here]).astype(bf16).astype(f32)
-        along = (col[:, here].astype(f32) - 0.5 + fc - width / 2).astype(bf16).astype(f32)
-        across = (row[:, here].astype(f32) - 0.5 + fr - depth / 2).astype(bf16).astype(f32)
+        departure[:, here] = flag[:, here].astype(f32) * innov
+        under = (lanes - members, lanes)
+        under = jnp.where(iota(under, 0) == 0, innov, 0.0).astype(bf16)
+        pert[here, :] = jnp.concatenate([rounded, under], axis=0).T
         values = rounded.astype(f32)
         for a in range(3):
-            u = (along - SHIFTS[a] * width) / width
             for c in range(3):
-                w = (across - SHIFTS[c] * depth) / depth
-                weight = gain * jnp.exp(-0.5 * (u * u + w * w))
-                weighted[a, c * members : (c + 1) * members, here] = (values * weight).astype(bf16)
+                k = 4 + a * 3 + c
+                weighted[a, c * members : (c + 1) * members, here] = (
+                    values * shares[k : k + 1, here]
+                ).astype(bf16)
         return carry
 
     lax.fori_loop(0, observations // lanes, block, 0, unroll=2)
 
     sums_copies = []
     for a in (0, 2, 1):
-        own[a] = dot_t(weighted[a], pert[...])
+        own[a] = jnp.dot(weighted[a], pert[...], preferred_element_type=f32)
         for c in (0, 2, 1):
             if a != 1 or c != 1:
                 sums_copies.append(
@@ -397,13 +434,13 @@
     stride = width + 8
     total = (depth + 1) * levels
     inner = (depth - 1) * levels
-    chunks = math.gcd(levels, 8)
+    chunks, parts = 4, 4
     lines = [
         x.reshape(1, observations)
         for x in (obs_level, obs_row, obs_col, frac_row, frac_col, obs_value, obs_error, obs_flag)
     ]
     vmem = pl.BlockSpec(memory_space=pltpu.VMEM)
-    anywhere = pl.BlockSpec(memory_space=pl.ANY)
+    outside = pl.BlockSpec(memory_space=pltpu.HBM)
     dma = pltpu.SemaphoreType.DMA
     sums, departure = pl.pallas_call(
         functools.partial(observe, n_lon, n_lat),
@@ -411,30 +448,32 @@
             jax.ShapeDtypeStruct((members, 128), f32),
             jax.ShapeDtypeStruct((1, observations), f32),
         ),
-        in_specs=[anywhere] * 9,
+        in_specs=[outside] * 9,
         out_specs=(vmem, vmem),
         scratch_shapes=[pltpu.VMEM(line.shape, line.dtype) for line in lines]
         + [
             pltpu.VMEM((1, observations), jnp.int32),
+            pltpu.VMEM((16, observations), f32),
             pltpu.VMEM(background.shape, bf16),
-            pltpu.VMEM((members * depth, width), f32),
+            pltpu.VMEM((levels, members * depth, width), f32),
             pltpu.VMEM((2, levels * members, width), bf16),
             pltpu.VMEM((2, levels * members, width), bf16),
             pltpu.VMEM((total * stride + 8, 2 * members), f32),
             pltpu.VMEM((2, inner, 2 * members), bf16),
             pltpu.VMEM((2, inner, 2 * members), bf16),
             pltpu.VMEM((2, 2, levels, 2 * members), bf16),
+            pltpu.VMEM((2, 2, levels, 2 * members), bf16),
             pltpu.SMEM((1, observations), jnp.int32),
             pltpu.VMEM((2 * observations, 2 * members), f32),
-            pltpu.VMEM((128, observations), bf16),
+            pltpu.VMEM((observations, 128), bf16),
             pltpu.VMEM((3, 3 * members, observations), bf16),
             pltpu.VMEM((3, 3 * members, 128), f32),
             pltpu.VMEM((3, 3, members, 128), f32),
             dma((chunks,)),
             dma((8,)),
             dma,
-            dma((2, chunks)),
-            dma((2, chunks)),
+            dma((2, parts)),
+            dma((2, parts)),
             dma((2,)),
             dma((2,)),
             dma((2, 2)),
@@ -443,7 +482,7 @@
             dma((3, 3)),
         ],
         compiler_params=pltpu.CompilerParams(
-            collective_id=0, has_side_effects=True, vmem_limit_bytes=48 << 20
+            collective_id=0, has_side_effects=True, vmem_limit_bytes=64 << 20
         ),
         name="observe",
     )(background, *lines)
@@ -454,8 +493,8 @@
             jax.ShapeDtypeStruct(background.shape, bf16),
             jax.ShapeDtypeStruct(departure.shape, f32),
         ),
-        in_specs=[vmem, vmem, vmem, anywhere],
-        out_specs=(anywhere, vmem),
+        in_specs=[vmem, vmem, vmem, outside],
+        out_specs=(outside, vmem),
         scratch_shapes=[
             pltpu.VMEM(background.shape, bf16),
             pltpu.VMEM(background.shape, bf16),
@@ -463,7 +502,7 @@
             dma((8,)),
             dma((levels // 2,)),
         ],
-        compiler_params=pltpu.CompilerParams(vmem_limit_bytes=40 << 20),
+        compiler_params=pltpu.CompilerParams(vmem_limit_bytes=64 << 20),
         name="update",
     )(sums, ocean, departure, background)
     return analysis, departure.reshape(obs_value.shape)

time: 48 us -> 38.4 us (0.80)
  local copies, waits for them, and re-layouts: 7.76 us -> 0 us
  Pallas kernels: 39 us -> 37.6 us
    unnamed x20 -> x0, local copies, waits for them, and re-layouts: 7.76 us -> none
    pallas_call x1, Pallas kernels: 30.7 us -> 28.8 us  [on_device(): pl.pallas_call(functools.partial(observe, n_lon, n_lat), out_shape=(jax.S...]
    pallas_call x1, Pallas kernels: 8.28 us -> 8.79 us  [on_device(): pl.pallas_call(update, out_shape=(jax.ShapeDtypeStruct(background.shape,...]
where the time goes in v2:
time: 38.4 us; the launch traced here: 38.3 us
  Pallas kernels  37.6 us (98%)
  between operations  0.64 us (2%)
    pallas_call x1, Pallas kernels, on_device(): pl.pallas_call(functools.partial(observe, n_lon, n_lat), out_shape=(jax.S...  28.8 us
    pallas_call x1, Pallas kernels, on_device(): pl.pallas_call(update, out_shape=(jax.ShapeDtypeStruct(background.shape,...  8.79 us

profile of v2, /device:TPU:1, one launch (start us, length us, event | category | flops | bytes accessed | tf_op | source)
XLA Modules:
  0.0 38.3 jit_solution(14914539441633546445)
XLA Ops:
  0.6 28.8 %observe.1 = (f32[64,128]{1,0:T(8,128)}, f32[1,2048]{1,0:T(1,128)}) custom-call(bf16[64,16,16,128]{3,2,1,0:T(8,128)(2,1)} %background.3, s32[1,2048]{1,0:T(1,128)} %bitcast.9, s32[1,2048]{1,0:T(1,128)} %bitcast.10, s32[1,2048]{1,0:T(1,128)} %bitcast.11, f32[1,2048]{1,0:T(1,128)} %bitcast.12, f32[1,2048]{1,0:T(1,128)} %bitcast.13, f32[1,2048]{1,0:T(1,128)} %bitcast.14, ...), custom_call_target="tpu_custom_call" | custom-call | tf_op jit(solution)/shard_map/observe/pallas_call | solution.py:445
  29.5 8.8 %update.1 = (bf16[64,16,16,128]{3,2,1,0:T(8,128)(2,1)}, f32[1,2048]{1,0:T(1,128)}) custom-call(f32[64,128]{1,0:T(8,128)} %get-tuple-element.6.sums, s32[16,128]{1,0:T(8,128)} %ocean.1, f32[1,2048]{1,0:T(1,128)} %get-tuple-element.7.departure, bf16[64,16,16,128]{3,2,1,0:T(8,128)(2,1)} %background.3), custom_call_target="tpu_custom_call" | custom-call | tf_op jit(solution)/shard_map/update/pallas_call | solution.py:490

commit v3 on v2

--- a/solution.py
+++ b/solution.py
@@ -302,7 +302,7 @@
                 ).astype(bf16)
         return carry
 
-    lax.fori_loop(0, observations // lanes, block, 0, unroll=2)
+    lax.fori_loop(0, observations // lanes, block, 0, unroll=4)
 
     sums_copies = []
     for a in (0, 2, 1):
@@ -347,7 +347,7 @@
 
 
 def update(
-    sums, ocean, departure, background, analysis, departure_out, held, result, spread_by, load_sem, store_sem
+    sums, ocean, departure, background, analysis, departure_out, held, result, spread_by, water_held, load_sem, store_sem, small_sem
 ):
     members, levels, depth, width = background.shape
     half = 8
@@ -363,7 +363,12 @@
     ]
     for load in loads:
         load.start()
-    departure_out[...] = departure[...]
+    smalls = [
+        pltpu.make_async_copy(ocean, water_held, small_sem.at[0]),
+        pltpu.make_async_copy(departure, departure_out, small_sem.at[1]),
+    ]
+    for copy in smalls:
+        copy.start()
     transform = transform_of(sums[...], members)
     shift = half.bit_length() - 1
     down = (jnp.right_shift(iota((n, members), 0), shift) == iota((n, members), 1)).astype(f32)
@@ -374,7 +379,9 @@
     spread_by[...] = jnp.where(same, wide, 0.0).astype(bf16)
     for load in loads:
         load.wait()
-    water = ocean[...] > 0
+    for copy in smalls:
+        copy.wait()
+    water = water_held[...] > 0
     at_once = 2
 
     def store(step):
@@ -493,14 +500,16 @@
             jax.ShapeDtypeStruct(background.shape, bf16),
             jax.ShapeDtypeStruct(departure.shape, f32),
         ),
-        in_specs=[vmem, vmem, vmem, outside],
-        out_specs=(outside, vmem),
+        in_specs=[vmem, outside, outside, outside],
+        out_specs=(outside, outside),
         scratch_shapes=[
             pltpu.VMEM(background.shape, bf16),
             pltpu.VMEM(background.shape, bf16),
             pltpu.VMEM((n, n), bf16),
+            pltpu.VMEM(ocean.shape, ocean.dtype),
             dma((8,)),
             dma((levels // 2,)),
+            dma((2,)),
         ],
         compiler_params=pltpu.CompilerParams(vmem_limit_bytes=64 << 20),
         name="update",

time: 38.4 us -> 37.5 us (0.977)
  Pallas kernels: 37.6 us -> 36.7 us
    pallas_call x1, Pallas kernels: 8.79 us -> 8.18 us  [on_device(): pl.pallas_call(update, out_shape=(jax.ShapeDtypeStruct(background.shape,...]
where the time goes in v3:
time: 37.5 us; the launch traced here: 37.3 us
  Pallas kernels  36.7 us (98%)
  between operations  0.64 us (2%)
    pallas_call x1, Pallas kernels, on_device(): pl.pallas_call(functools.partial(observe, n_lon, n_lat), out_shape=(jax.S...  28.5 us
    pallas_call x1, Pallas kernels, on_device(): pl.pallas_call(update, out_shape=(jax.ShapeDtypeStruct(background.shape,...  8.18 us

profile of v3, /device:TPU:1, one launch (start us, length us, event | category | flops | bytes accessed | tf_op | source)
XLA Modules:
  0.0 37.3 jit_solution(1047240300668911365)
XLA Ops:
  0.6 28.5 %observe.1 = (f32[64,128]{1,0:T(8,128)}, f32[1,2048]{1,0:T(1,128)}) custom-call(bf16[64,16,16,128]{3,2,1,0:T(8,128)(2,1)} %background.3, s32[1,2048]{1,0:T(1,128)} %bitcast.9, s32[1,2048]{1,0:T(1,128)} %bitcast.10, s32[1,2048]{1,0:T(1,128)} %bitcast.11, f32[1,2048]{1,0:T(1,128)} %bitcast.12, f32[1,2048]{1,0:T(1,128)} %bitcast.13, f32[1,2048]{1,0:T(1,128)} %bitcast.14, ...), custom_call_target="tpu_custom_call" | custom-call | tf_op jit(solution)/shard_map/observe/pallas_call | solution.py:452
  29.1 8.2 %update.1 = (bf16[64,16,16,128]{3,2,1,0:T(8,128)(2,1)}, f32[1,2048]{1,0:T(1,128)}) custom-call(f32[64,128]{1,0:T(8,128)} %get-tuple-element.6.sums, s32[16,128]{1,0:T(8,128)} %ocean.1, f32[1,2048]{1,0:T(1,128)} %get-tuple-element.7.departure, bf16[64,16,16,128]{3,2,1,0:T(8,128)(2,1)} %background.3), custom_call_target="tpu_custom_call" | custom-call | tf_op jit(solution)/shard_map/update/pallas_call | solution.py:497
